TPU v7x, 256 devices: a whole 4x4x8 slice. The times are simulated.
256 devices in a mesh: snp: 32 (over y, z), ind: 8 (over x, core).
Axes of the slice: x: 4, y: 4, z: 8, core: 2. Of those that a mesh axis runs over, the one named last changes fastest.
Arguments:
- beta_hat: float32 [64, 32768], P('ind', 'snp'), may hold values from -8 to 8
- ld_band: float32 [32768, 1024], P('snp'), as said below
- band_start: int32 [256], P('snp'), may hold values from -480 to 32224, as said below
- heritability: float32 [64], P('ind'), may hold values from 0.2 to 0.6
- genotypes: bfloat16 [8192, 32768], P('ind', 'snp'), may hold values from 0 to 2, as said below
Outputs:
- weights: float32 [64, 32768], P('ind', 'snp')
- scores: float32 [64, 8192], P(None, ('ind', 'snp'))
Inputs may be any that keep to these rules, and one draw needn't show every extreme that they name: ld_band is a symmetric matrix R in band form: entry k of row i is R[i, band_start[i // 128] + k]; R[i, i] = 1; R[i, j] = 0 when |i - j| > 416 or j lies outside the SNPs; the off-diagonal magnitudes of a row sum to 2.5 at most. `band_start`: block b's window starts at 128 * b - 416 - k with k from 0 to 64; the first block has k = 64 and the last block k = 0. `genotypes`: dosages are 0, 1 or 2.
All inputs are finite; a program needn't handle non-finite values.
Results may differ from a plain program's by a relative error of at most 0.0021.
Values may be sent and summed in bfloat16 or wider, within the bound.
A program may use at most 64 MiB of HBM per device.

v0:
```python
import jax
import jax.numpy as jnp
from jax import lax
from jax.sharding import PartitionSpec as P

BLK = 128
ITERS = 2
M_GENOME = 1100000
N_GWAS = 1000000


def padded_2(block, sides, width):
    for axis, dim in sides:
        count = lax.axis_size(axis)
        forward = [(i, i + 1) for i in range(count - 1)]
        backward = [(target, source) for source, target in forward]
        low = lax.ppermute(
            lax.slice_in_dim(block, block.shape[dim] - width, None, axis=dim), axis, forward
        )
        high = lax.ppermute(lax.slice_in_dim(block, 0, width, axis=dim), axis, backward)
        block = jnp.concatenate([low, block, high], axis=dim)
    return block


def apply_operator(vector, ld_band, band_start, ridge_shift):
    band_cols = ld_band.shape[1]
    halo_cols = band_cols - BLK
    padded = padded_2(vector, (("snp", 1),), halo_cols)
    local_rows = vector.shape[1]
    offsets = band_start - lax.axis_index("snp") * local_rows + halo_cols
    windows = jax.vmap(lambda row_begin: lax.dynamic_slice_in_dim(padded, row_begin, band_cols, 1))(
        offsets
    )
    blocks = ld_band.reshape(band_start.shape[0], BLK, band_cols)
    product = jnp.einsum("btk,brk->tbr", windows, blocks, precision=lax.Precision.HIGHEST)
    return product.reshape(vector.shape) + ridge_shift[:, None] * vector


def norm_sum(residual):
    return lax.psum(jnp.sum(residual * residual, axis=1), "snp")


def local(beta_hat, ld_band, band_start, heritability, genotypes):
    ridge_shift = M_GENOME / N_GWAS / heritability
    weights = jnp.zeros_like(beta_hat)
    residual = beta_hat
    direction = beta_hat
    norm_now = norm_sum(residual)
    for turn_index in range(ITERS):
        product = apply_operator(direction, ld_band, band_start, ridge_shift)
        curved = lax.psum(jnp.sum(direction * product, axis=1), "snp")
        step_size = norm_now / curved
        weights = weights + step_size[:, None] * direction
        residual = residual - step_size[:, None] * product
        if turn_index + 1 < ITERS:
            norm_next = norm_sum(residual)
            direction = residual + (norm_next / norm_now)[:, None] * direction
            norm_now = norm_next
    rounded = weights.astype(jnp.bfloat16)
    partial_scores = lax.dot_general(
        lax.all_gather(rounded, "ind", axis=0, tiled=True),
        genotypes,
        (((1,), (1,)), ((), ())),
        preferred_element_type=jnp.float32,
    )
    complete = lax.psum(partial_scores, "snp")
    count = complete.shape[1] * lax.axis_size("ind")
    summed = lax.psum(jnp.sum(complete, axis=1), "ind")
    average = summed / count
    centred = complete - average[:, None]
    variance = lax.psum(jnp.sum(centred * centred, axis=1), "ind") / count
    share_cols = complete.shape[1] // lax.axis_size("snp")
    own_part = lax.dynamic_slice_in_dim(centred, lax.axis_index("snp") * share_cols, share_cols, 1)
    scores = own_part * lax.rsqrt(variance + 1e-05)[:, None]
    return (weights, scores)


def solution(mesh):
    placed = (P("ind", "snp"), P("snp", None), P("snp"), P("ind"), P("ind", "snp"))
    return jax.shard_map(
        local,
        mesh=mesh,
        in_specs=placed,
        out_specs=(P("ind", "snp"), P(None, ("ind", "snp"))),
        check_vma=False,
    )
```

profile of v0, /device:TPU:1, one launch (start us, length us, event | category | flops | bytes accessed | tf_op | source)
XLA Modules:
  0.0 465.0 jit_solution(3514487914134571717)
XLA Ops:
  7.2 0.9 fusion.7
  8.1 4.4 collective-permute-start
  12.5 1.3 collective-permute-start.1
  15.2 2.2 collective-permute-done.1
  17.3 0.8 pad_maximum_fusion
  18.1 10.5 %while.2 = (s32[]{:T(128)}, f32[8,2816]{1,0:T(8,128)S(1)}, s32[8,2]{0,1:T(2,128)S(1)}, f32[8,8,1024]{2,1,0:T(8,128)S(1)}, s32[]{:T(128)}) while((s32[]{:T(128)}, f32[8,2816]{1,0:T(8,128)S(1)}, s32[8,2]{0,1:T(2,128)S(1)}, f32[8,8,1024]{2,1,0:T(8,128)S(1)}, s32[]{:T(128)}) %tuple.38), condition=%wide.while_cond, body=%wide.while_body.sunk | while | flops 2 | bytes 65633 | solution.py:31
  18.7 0.7 bitcast_dynamic-update-slice_fusion.4
  20.0 0.7 bitcast_dynamic-update-slice_fusion.4
  21.3 0.7 bitcast_dynamic-update-slice_fusion.4
  22.7 0.7 bitcast_dynamic-update-slice_fusion.4
  24.0 0.7 bitcast_dynamic-update-slice_fusion.4
  25.3 0.7 bitcast_dynamic-update-slice_fusion.4
  26.6 0.7 bitcast_dynamic-update-slice_fusion.4
  27.9 0.7 bitcast_dynamic-update-slice_fusion.4
  28.6 5.4 %multiply_reduce_fusion.2 = (f32[8]{0:T(128)S(1)}, f32[8]{0:T(128)S(1)}, f32[8,1024]{1,0:T(8,128)S(1)}) fusion(f32[8,1024]{1,0:T(8,128)} %param.5, f32[8]{0:T(128)S(1)} %broadcast_divide_fusion, f32[8,8,1024]{2,1,0:T(8,128)S(1)} %get-tuple-element.9, f32[8,128,1024]{2,1,0:T(8,128)} %bitcast.39), kind=kOutput, calls=%fused_computation.19 | convolution fusion | flops 100712432 | bytes 4522080 | tf_op jit(solution)/shard_map/btk,brk->tbr/dot_general | solution.py:35
  34.1 62.4 %all-reduce.1 = (f32[8]{0:T(128)S(1)}, f32[8]{0:T(128)S(1)}) all-reduce(f32[8]{0:T(128)S(1)} %get-tuple-element.21, f32[8]{0:T(128)S(1)} %get-tuple-element.20), channel_id=1, replica_groups=mesh['snp'=32,'ind'=8] {'snp'}, use_global_device_ids=true, to_apply=%region_1.0 | all-reduce | flops 16 | bytes 128 | tf_op jit(solution)/shard_map/psum | solution.py:40
  96.6 55.7 %psum.51 = f32[8]{0:T(128)S(1)} all-reduce(f32[8]{0:T(128)S(1)} %multiply_reduce_fusion.1), channel_id=1, replica_groups=mesh['snp'=32,'ind'=8] {'snp'}, use_global_device_ids=true, to_apply=%region_5.0 | all-reduce | flops 8 | bytes 64 | tf_op jit(solution)/shard_map/psum | solution.py:40
  152.5 3.6 collective-permute-start.2
  156.0 1.3 collective-permute-start.3
  157.3 3.6 collective-permute-done.3
  161.0 10.5 %while.3 = (s32[]{:T(128)}, f32[8,2816]{1,0:T(8,128)S(1)}, s32[8,2]{0,1:T(2,128)S(1)}, f32[8,8,1024]{2,1,0:T(8,128)S(1)}, s32[]{:T(128)}) while((s32[]{:T(128)}, f32[8,2816]{1,0:T(8,128)S(1)}, s32[8,2]{0,1:T(2,128)S(1)}, f32[8,8,1024]{2,1,0:T(8,128)S(1)}, s32[]{:T(128)}) %tuple.46), condition=%wide.while_cond.1, body=%wide.while_body.1.sunk | while | flops 2 | bytes 65633 | solution.py:31
  161.6 0.7 bitcast_dynamic-update-slice_fusion.5
  162.9 0.7 bitcast_dynamic-update-slice_fusion.5
  171.5 5.4 %fusion.3 = f32[8]{0:T(128)S(1)} fusion(f32[8,1024]{1,0:T(8,128)S(1)} %multiply_add_fusion.1, f32[8,8,1024]{2,1,0:T(8,128)S(1)} %get-tuple-element.17, f32[8,128,1024]{2,1,0:T(8,128)} %bitcast.40, f32[8]{0:T(128)S(1)} %broadcast_divide_fusion), kind=kOutput, calls=%fused_computation.9 | convolution fusion | flops 100696056 | bytes 4489280 | tf_op jit(solution)/shard_map/btk,brk->tbr/dot_general | solution.py:35
  176.9 55.7 %psum.52 = f32[8]{0:T(128)S(1)} all-reduce(f32[8]{0:T(128)S(1)} %fusion.3), channel_id=1, replica_groups=mesh['snp'=32,'ind'=8] {'snp'}, use_global_device_ids=true, to_apply=%region_7.0 | all-reduce | flops 8 | bytes 64 | tf_op jit(solution)/shard_map/psum | solution.py:51
  233.3 57.2 %all_gather.3 = bf16[64,1024]{1,0:T(8,128)(2,1)S(1)} all-gather(bf16[8,1024]{1,0:T(8,128)(2,1)S(1)} %get-tuple-element.42), channel_id=1, replica_groups=mesh['snp'=32,'ind'=8] {'ind'}, dimensions={0}, use_global_device_ids=true | all-gather | bytes 147456 | tf_op jit(solution)/shard_map/all_gather | solution.py:61
  290.5 1.5 fusion.8
  292.0 133.9 %all-reduce.4.cloned.1.call-done = f32[64,1024]{1,0:T(8,128)} async-done(((f32[64,1024]{1,0:T(8,128)}), f32[64,1024]{1,0:T(8,128)}) %all-reduce.4.cloned.1.call-update) | async-done | bytes 262160 | tf_op jit(solution)/shard_map/psum | solution.py:66
  425.9 1.1 reduce_sum.58
  426.9 16.9 %psum.54 = f32[64]{0:T(128)S(1)} all-reduce(f32[64]{0:T(128)S(1)} %reduce_sum.58), channel_id=1, replica_groups=mesh['snp'=32,'ind'=8] {'ind'}, use_global_device_ids=true, to_apply=%region_10.0 | all-reduce | flops 64 | bytes 512 | tf_op jit(solution)/shard_map/psum | solution.py:68
  443.8 1.1 multiply_reduce_fusion
  445.0 12.4 %psum.55 = f32[64]{0:T(128)S(1)} all-reduce(f32[64]{0:T(128)S(1)} %get-tuple-element.40), channel_id=1, replica_groups=mesh['snp'=32,'ind'=8] {'ind'}, use_global_device_ids=true, to_apply=%region_12.0 | all-reduce | flops 64 | bytes 512 | tf_op jit(solution)/shard_map/psum | solution.py:71
  (63 shorter events, 17.0 us)
Async XLA Ops:
  7.2 283.4 %copy-start = (bf16[1024,1024]{1,0:T(8,128)(2,1)S(1)}, bf16[1024,1024]{1,0:T(8,128)(2,1)}, u32[]{:S(2)}) copy-start(bf16[1024,1024]{1,0:T(8,128)(2,1)} %param.9) | copy-start | bytes 6291460
  7.2 89.3 %copy-start.1 = (f32[8,1024]{1,0:T(8,128)S(1)}, f32[8,1024]{1,0:T(8,128)}, u32[]{:S(2)}) copy-start(f32[8,1024]{1,0:T(8,128)} %param.5) | copy-start | bytes 98308
  7.2 418.7 %all-reduce.4.cloned.1.call-start = ((), (), s32[]{:S(2)}) async-start(), calls=%async_computation | async-start | bytes 524288 | tf_op jit(solution)/shard_map/psum | solution.py:66
  8.1 7.0 %collective-permute-start = (f32[8,896]{1,0:T(8,128)S(1)}, f32[8,896]{1,0:T(8,128)S(1)}, u32[]{:S(2)}, u32[]{:S(2)}) collective-permute-start(f32[8,896]{1,0:T(8,128)S(1)} %get-tuple-element.46), channel_id=1, source_target_pairs={{0,8},{8,16},{16,24},{24,32},{32,40},{40,48},{48,56},{56,64},{64,7... | collective-permute-start | bytes 86024 | tf_op jit(solution)/shard_map/ppermute | solution.py:17
  12.5 4.8 %collective-permute-start.1 = (f32[8,896]{1,0:T(8,128)S(1)}, f32[8,896]{1,0:T(8,128)S(1)}, u32[]{:S(2)}, u32[]{:S(2)}) collective-permute-start(f32[8,896]{1,0:T(8,128)S(1)} %get-tuple-element.47), channel_id=1, source_target_pairs={{8,0},{16,8},{24,16},{32,24},{40,32},{48,40},{56,48},{64,56},{72,6... | collective-permute-start | bytes 86024 | tf_op jit(solution)/shard_map/ppermute | solution.py:20
  152.5 4.9 %collective-permute-start.2 = (f32[8,896]{1,0:T(8,128)S(1)}, f32[8,896]{1,0:T(8,128)S(1)}, u32[]{:S(2)}, u32[]{:S(2)}) collective-permute-start(f32[8,896]{1,0:T(8,128)S(1)} %get-tuple-element.44), channel_id=1, source_target_pairs={{0,8},{8,16},{16,24},{24,32},{32,40},{40,48},{48,56},{56,64},{64,7... | collective-permute-start | bytes 86024 | tf_op jit(solution)/shard_map/ppermute | solution.py:17
  156.0 4.9 %collective-permute-start.3 = (f32[8,896]{1,0:T(8,128)S(1)}, f32[8,896]{1,0:T(8,128)S(1)}, u32[]{:S(2)}, u32[]{:S(2)}) collective-permute-start(f32[8,896]{1,0:T(8,128)S(1)} %get-tuple-element.45), channel_id=1, source_target_pairs={{8,0},{16,8},{24,16},{32,24},{40,32},{48,40},{56,48},{64,56},{72,6... | collective-permute-start | bytes 86024 | tf_op jit(solution)/shard_map/ppermute | solution.py:20
Sparse Core Ops, SparseCore 0:
  292.1 133.6 all-reduce.3
where the time goes:
time: 466 us; the launch traced here: 465 us
  blocking collectives  260 us (56%)
  waiting for transfers between devices  140 us (30%)
  local copies, waits for them, and re-layouts  22.7 us (5%)
  between operations  14.1 us (3%)
  matrix products  12.3 us (3%)
  starting transfers between devices  10.5 us (2%)
  other arithmetic  5.4 us (1%)
    psum x1, waiting for transfers between devices, local(): complete = lax.psum(partial_scores, 'snp')  134 us
    psum x2, blocking collectives, norm_sum(): return lax.psum(jnp.sum(residual * residual, axis=1), 'snp')  118 us
    all_gather x1, blocking collectives, local(): lax.all_gather(rounded, 'ind', axis=0, tiled=True)  57.2 us
    psum x1, blocking collectives, local(): curved = lax.psum(jnp.sum(direction * product, axis=1), 'snp')  55.7 us
    gather x48, local copies, waits for them, and re-layouts  21 us
    psum x1, blocking collectives, local(): summed = lax.psum(jnp.sum(complete, axis=1), 'ind')  16.9 us
    psum x1, blocking collectives, local(): variance = lax.psum(jnp.sum(centred * centred, axis=1), 'ind') / count  12.4 us
    dot_general x2, matrix products, apply_operator(): jnp.einsum('btk,brk->tbr', windows, blocks, precision=lax.Precision.HIGHEST)  10.8 us
  transfers between devices with their start and end apart: 5, of which 3 were waited for; matrix products, arithmetic and copies ran while one was open for 0% of the time, Pallas kernels for 0%

commit v1 on v0

--- a/solution.py
+++ b/solution.py
@@ -63,7 +63,7 @@
         (((1,), (1,)), ((), ())),
         preferred_element_type=jnp.float32,
     )
-    complete = lax.psum(partial_scores, "snp")
+    complete = jnp.sum(lax.all_gather(partial_scores, "snp"), axis=0)
     count = complete.shape[1] * lax.axis_size("ind")
     summed = lax.psum(jnp.sum(complete, axis=1), "ind")
     average = summed / count

time: 466 us -> 428 us (0.918)
  waiting for transfers between devices: 140 us -> 98.1 us
  other arithmetic: 5.4 us -> 11.2 us
    psum x1 -> x0, waiting for transfers between devices: 134 us -> none  [local(): complete = lax.psum(partial_scores, 'snp')]
    all_gather x0 -> x1, waiting for transfers between devices: none -> 92.3 us  [local(): complete = jnp.sum(lax.all_gather(partial_scores, 'snp'), axis=0)]
where the time goes in v1:
time: 428 us; the launch traced here: 427 us
  blocking collectives  258 us (60%)
  waiting for transfers between devices  98.1 us (23%)
  local copies, waits for them, and re-layouts  22.7 us (5%)
  between operations  14.1 us (3%)
  matrix products  12.3 us (3%)
  other arithmetic  11.2 us (3%)
  starting transfers between devices  10.5 us (2%)
    psum x2, blocking collectives, norm_sum(): return lax.psum(jnp.sum(residual * residual, axis=1), 'snp')  118 us
    all_gather x1, waiting for transfers between devices, local(): complete = jnp.sum(lax.all_gather(partial_scores, 'snp'), axis=0)  92.3 us
    all_gather x1, blocking collectives, local(): lax.all_gather(rounded, 'ind', axis=0, tiled=True)  57.2 us
    psum x1, blocking collectives, local(): curved = lax.psum(jnp.sum(direction * product, axis=1), 'snp')  55.7 us
    gather x48, local copies, waits for them, and re-layouts  21 us
    psum x1, blocking collectives, local(): variance = lax.psum(jnp.sum(centred * centred, axis=1), 'ind') / count  14.1 us
    psum x1, blocking collectives, local(): summed = lax.psum(jnp.sum(complete, axis=1), 'ind')  12.9 us
    dot_general x2, matrix products, apply_operator(): jnp.einsum('btk,brk->tbr', windows, blocks, precision=lax.Precision.HIGHEST)  10.8 us
  transfers between devices with their start and end apart: 5, of which 3 were waited for; matrix products, arithmetic and copies ran while one was open for 0% of the time, Pallas kernels for 0%

profile of v1, /device:TPU:1, one launch (start us, length us, event | category | flops | bytes accessed | tf_op | source)
XLA Modules:
  0.0 427.0 jit_solution(4329994094951306491)
XLA Ops:
  7.2 0.9 fusion.7
  8.1 4.4 %collective-permute-start = (f32[8,896]{1,0:T(8,128)S(1)}, f32[8,896]{1,0:T(8,128)S(1)}, u32[]{:S(2)}, u32[]{:S(2)}) collective-permute-start(f32[8,896]{1,0:T(8,128)S(1)} %get-tuple-element.48), channel_id=1, source_target_pairs={{0,8},{8,16},{16,24},{24,32},{32,40},{40,48},{48,56},{56,64},{64,7... | collective-permute-start | bytes 86024 | tf_op jit(solution)/shard_map/ppermute | solution.py:17
  12.5 1.3 collective-permute-start.1
  15.2 2.2 collective-permute-done.1
  17.3 0.8 pad_maximum_fusion
  18.1 10.5 %while.2 = (s32[]{:T(128)}, f32[8,2816]{1,0:T(8,128)S(1)}, s32[8,2]{0,1:T(2,128)S(1)}, f32[8,8,1024]{2,1,0:T(8,128)S(1)}, s32[]{:T(128)}) while((s32[]{:T(128)}, f32[8,2816]{1,0:T(8,128)S(1)}, s32[8,2]{0,1:T(2,128)S(1)}, f32[8,8,1024]{2,1,0:T(8,128)S(1)}, s32[]{:T(128)}) %tuple.39), condition=%wide.while_cond, body=%wide.while_body.sunk | while | flops 2 | bytes 65641 | solution.py:31
  18.7 0.7 bitcast_dynamic-update-slice_fusion.4
  20.0 0.7 bitcast_dynamic-update-slice_fusion.4
  21.3 0.7 bitcast_dynamic-update-slice_fusion.4
  22.7 0.7 bitcast_dynamic-update-slice_fusion.4
  24.0 0.7 bitcast_dynamic-update-slice_fusion.4
  25.3 0.7 bitcast_dynamic-update-slice_fusion.4
  26.6 0.7 bitcast_dynamic-update-slice_fusion.4
  27.9 0.7 bitcast_dynamic-update-slice_fusion.4
  28.6 5.4 %multiply_reduce_fusion.2 = (f32[8]{0:T(128)S(1)}, f32[8]{0:T(128)S(1)}, f32[8,1024]{1,0:T(8,128)S(1)}) fusion(f32[8,1024]{1,0:T(8,128)} %param.5, f32[8]{0:T(128)S(1)} %broadcast_divide_fusion, f32[8,8,1024]{2,1,0:T(8,128)S(1)} %get-tuple-element.9, f32[8,128,1024]{2,1,0:T(8,128)} %bitcast.41), kind=kOutput, calls=%fused_computation.19 | convolution fusion | flops 100712432 | bytes 4522080 | tf_op jit(solution)/shard_map/btk,brk->tbr/dot_general | solution.py:35
  34.1 62.4 %all-reduce.1 = (f32[8]{0:T(128)S(1)}, f32[8]{0:T(128)S(1)}) all-reduce(f32[8]{0:T(128)S(1)} %get-tuple-element.23, f32[8]{0:T(128)S(1)} %get-tuple-element.22), channel_id=1, replica_groups=mesh['snp'=32,'ind'=8] {'snp'}, use_global_device_ids=true, to_apply=%region_1.0 | all-reduce | flops 16 | bytes 128 | tf_op jit(solution)/shard_map/psum | solution.py:40
  96.6 55.7 %psum.44 = f32[8]{0:T(128)S(1)} all-reduce(f32[8]{0:T(128)S(1)} %multiply_reduce_fusion.1), channel_id=1, replica_groups=mesh['snp'=32,'ind'=8] {'snp'}, use_global_device_ids=true, to_apply=%region_5.0 | all-reduce | flops 8 | bytes 64 | tf_op jit(solution)/shard_map/psum | solution.py:40
  152.5 3.6 collective-permute-start.2
  156.0 1.3 collective-permute-start.3
  157.3 3.6 collective-permute-done.3
  161.0 10.5 %while.3 = (s32[]{:T(128)}, f32[8,2816]{1,0:T(8,128)S(1)}, s32[8,2]{0,1:T(2,128)S(1)}, f32[8,8,1024]{2,1,0:T(8,128)S(1)}, s32[]{:T(128)}) while((s32[]{:T(128)}, f32[8,2816]{1,0:T(8,128)S(1)}, s32[8,2]{0,1:T(2,128)S(1)}, f32[8,8,1024]{2,1,0:T(8,128)S(1)}, s32[]{:T(128)}) %tuple.47), condition=%wide.while_cond.1, body=%wide.while_body.1.sunk | while | flops 2 | bytes 65641 | solution.py:31
  161.6 0.7 bitcast_dynamic-update-slice_fusion.5
  162.9 0.7 bitcast_dynamic-update-slice_fusion.5
  171.5 5.4 %fusion.3 = f32[8]{0:T(128)S(1)} fusion(f32[8,1024]{1,0:T(8,128)S(1)} %multiply_add_fusion.1, f32[8,8,1024]{2,1,0:T(8,128)S(1)} %get-tuple-element.17, f32[8,128,1024]{2,1,0:T(8,128)} %bitcast.42, f32[8]{0:T(128)S(1)} %broadcast_divide_fusion), kind=kOutput, calls=%fused_computation.9 | convolution fusion | flops 100696056 | bytes 4489280 | tf_op jit(solution)/shard_map/btk,brk->tbr/dot_general | solution.py:35
  176.9 55.7 %psum.45 = f32[8]{0:T(128)S(1)} all-reduce(f32[8]{0:T(128)S(1)} %fusion.3), channel_id=1, replica_groups=mesh['snp'=32,'ind'=8] {'snp'}, use_global_device_ids=true, to_apply=%region_7.0 | all-reduce | flops 8 | bytes 64 | tf_op jit(solution)/shard_map/psum | solution.py:51
  233.3 57.2 %all_gather.9 = bf16[64,1024]{1,0:T(8,128)(2,1)S(1)} all-gather(bf16[8,1024]{1,0:T(8,128)(2,1)S(1)} %get-tuple-element.44), channel_id=1, replica_groups=mesh['snp'=32,'ind'=8] {'ind'}, dimensions={0}, use_global_device_ids=true | all-gather | bytes 147456 | tf_op jit(solution)/shard_map/all_gather | solution.py:61
  290.5 1.5 fusion.8
  292.0 92.3 %all-gather.3.cloned.1.call-done = f32[2048,1024]{1,0:T(8,128)} async-done(((f32[64,1024]{1,0:T(8,128)}), f32[2048,1024]{1,0:T(8,128)}) %all-gather.3.cloned.1.call-update) | async-done | bytes 8388624 | tf_op jit(solution)/shard_map/all_gather | solution.py:66
  384.3 3.8 reduce.1
  388.3 12.9 %psum.46 = f32[64]{0:T(128)S(1)} all-reduce(f32[64]{0:T(128)S(1)} %reduce_sum.68), channel_id=1, replica_groups=mesh['snp'=32,'ind'=8] {'ind'}, use_global_device_ids=true, to_apply=%region_10.0 | all-reduce | flops 64 | bytes 512 | tf_op jit(solution)/shard_map/psum | solution.py:68
  401.1 4.0 reduce_sum.67
  405.3 14.1 %psum.47 = f32[64]{0:T(128)S(1)} all-reduce(f32[64]{0:T(128)S(1)} %get-tuple-element.42), channel_id=1, replica_groups=mesh['snp'=32,'ind'=8] {'ind'}, use_global_device_ids=true, to_apply=%region_12.0 | all-reduce | flops 64 | bytes 512 | tf_op jit(solution)/shard_map/psum | solution.py:71
  (66 shorter events, 17.3 us)
Async XLA Ops:
  7.2 283.4 %copy-start = (bf16[1024,1024]{1,0:T(8,128)(2,1)S(1)}, bf16[1024,1024]{1,0:T(8,128)(2,1)}, u32[]{:S(2)}) copy-start(bf16[1024,1024]{1,0:T(8,128)(2,1)} %param.9) | copy-start | bytes 6291460
  7.2 89.3 %copy-start.1 = (f32[8,1024]{1,0:T(8,128)S(1)}, f32[8,1024]{1,0:T(8,128)}, u32[]{:S(2)}) copy-start(f32[8,1024]{1,0:T(8,128)} %param.5) | copy-start | bytes 98308
  7.2 377.1 %all-gather.3.cloned.1.call-start = ((), (), s32[]{:S(2)}) async-start(), calls=%async_computation | async-start | bytes 8650752 | tf_op jit(solution)/shard_map/all_gather | solution.py:66
  8.1 7.0 %collective-permute-start = (f32[8,896]{1,0:T(8,128)S(1)}, f32[8,896]{1,0:T(8,128)S(1)}, u32[]{:S(2)}, u32[]{:S(2)}) collective-permute-start(f32[8,896]{1,0:T(8,128)S(1)} %get-tuple-element.48), channel_id=1, source_target_pairs={{0,8},{8,16},{16,24},{24,32},{32,40},{40,48},{48,56},{56,64},{64,7... | collective-permute-start | bytes 86024 | tf_op jit(solution)/shard_map/ppermute | solution.py:17
  12.5 4.8 %collective-permute-start.1 = (f32[8,896]{1,0:T(8,128)S(1)}, f32[8,896]{1,0:T(8,128)S(1)}, u32[]{:S(2)}, u32[]{:S(2)}) collective-permute-start(f32[8,896]{1,0:T(8,128)S(1)} %get-tuple-element.49), channel_id=1, source_target_pairs={{8,0},{16,8},{24,16},{32,24},{40,32},{48,40},{56,48},{64,56},{72,6... | collective-permute-start | bytes 86024 | tf_op jit(solution)/shard_map/ppermute | solution.py:20
  152.5 4.9 %collective-permute-start.2 = (f32[8,896]{1,0:T(8,128)S(1)}, f32[8,896]{1,0:T(8,128)S(1)}, u32[]{:S(2)}, u32[]{:S(2)}) collective-permute-start(f32[8,896]{1,0:T(8,128)S(1)} %get-tuple-element.46), channel_id=1, source_target_pairs={{0,8},{8,16},{16,24},{24,32},{32,40},{40,48},{48,56},{56,64},{64,7... | collective-permute-start | bytes 86024 | tf_op jit(solution)/shard_map/ppermute | solution.py:17
  156.0 4.9 %collective-permute-start.3 = (f32[8,896]{1,0:T(8,128)S(1)}, f32[8,896]{1,0:T(8,128)S(1)}, u32[]{:S(2)}, u32[]{:S(2)}) collective-permute-start(f32[8,896]{1,0:T(8,128)S(1)} %get-tuple-element.47), channel_id=1, source_target_pairs={{8,0},{16,8},{24,16},{32,24},{40,32},{48,40},{56,48},{64,56},{72,6... | collective-permute-start | bytes 86024 | tf_op jit(solution)/shard_map/ppermute | solution.py:20
Sparse Core Ops, SparseCore 0:
  292.1 92.1 all-gather.2
